TPU v7x, 32 devices: a whole 2x2x4 slice. The times are simulated.
32 devices in a mesh: dp: 2 (over core), ctx: 4 (over y, x), tensor: 4 (over z).
Axes of the slice: x: 2, y: 2, z: 4, core: 2. Of those that a mesh axis runs over, the one named last changes fastest.
Arguments:
- hidden_in: bfloat16 [4, 1024, 2048], P('dp', 'ctx'), may hold values from -6 to 6
- segment_ids: int32 [4, 1024], P('dp', 'ctx'), may hold values from 0 to 21, as said below
- teacher: bfloat16 [4, 1024, 2048], P('dp', 'ctx'), may hold values from -6 to 6
- w_query: bfloat16 [2048, 2048], P(None, 'tensor'), may hold values from -0.125 to 0.125
- b_query: float32 [2048], P('tensor'), may hold values from -1.75 to 1.75
- w_key: bfloat16 [2048, 2048], P(None, 'tensor'), may hold values from -0.125 to 0.125
- w_value: bfloat16 [2048, 2048], P(None, 'tensor'), may hold values from -0.125 to 0.125
- b_value: float32 [2048], P('tensor'), may hold values from -1.75 to 1.75
- w_output: bfloat16 [2048, 2048], P('tensor'), may hold values from -0.75 to 0.75
- b_output: float32 [2048], replicated, may hold values from -1.75 to 1.75
- first_gain: float32 [2048], replicated, may hold values from 0.5 to 1.5
- first_shift: float32 [2048], replicated, may hold values from -1.75 to 1.75
- w_inner: bfloat16 [2048, 8192], P(None, 'tensor'), may hold values from -0.125 to 0.125
- b_inner: float32 [8192], P('tensor'), may hold values from -1.75 to 1.75
- w_outer: bfloat16 [8192, 2048], P('tensor'), may hold values from -0.09375 to 0.09375
- b_outer: float32 [2048], replicated, may hold values from -1.75 to 1.75
- second_gain: float32 [2048], replicated, may hold values from 0.5 to 1.5
- second_shift: float32 [2048], replicated, may hold values from -1.75 to 1.75
Outputs:
- layer_out: bfloat16 [4, 1024, 2048], P('dp', 'ctx')
- loss: float32 [], replicated
- grad_input: float32 [4, 1024, 2048], P('dp', 'ctx')
- grad_w_query: float32 [2048, 2048], P(('dp', 'ctx'), 'tensor')
- grad_b_query: float32 [2048], P('tensor')
- grad_w_key: float32 [2048, 2048], P(('dp', 'ctx'), 'tensor')
- grad_w_value: float32 [2048, 2048], P(('dp', 'ctx'), 'tensor')
- grad_b_value: float32 [2048], P('tensor')
- grad_w_output: float32 [2048, 2048], P('tensor', ('dp', 'ctx'))
- grad_b_output: float32 [2048], replicated
- grad_first_gain: float32 [2048], replicated
- grad_first_shift: float32 [2048], replicated
- grad_w_inner: float32 [2048, 8192], P(('dp', 'ctx'), 'tensor')
- grad_b_inner: float32 [8192], P('tensor')
- grad_w_outer: float32 [8192, 2048], P('tensor', ('dp', 'ctx'))
- grad_b_outer: float32 [2048], replicated
- grad_second_gain: float32 [2048], replicated
- grad_second_shift: float32 [2048], replicated
Inputs may be any that keep to these rules, and one draw needn't show every extreme that they name: `segment_ids`: in each sequence the documents are numbered 1, 2, 3 and so on in order, each of 51 to 512 tokens but the last, which may be cut by the padding tail of zeros at the sequence's end (1 to 128 tokens); in each group of 2 consecutive sequences one, drawn, is a single document 1 with no padding.
All inputs are finite; a program needn't handle non-finite values.
Results may differ from a plain program's by a relative error of at most 0.015.
Values may be sent and summed in bfloat16 or wider, within the bound.
A program may use at most 320 MiB of HBM per device.

v0:
```python
import jax
import jax.numpy as jnp
from jax import lax
from jax.sharding import PartitionSpec as P

HD = 128


def layer_norm(values, gain, shift):
    center = values - jnp.mean(values, axis=-1, keepdims=True)
    spread = jnp.mean(center * center, axis=-1, keepdims=True)
    return center * lax.rsqrt(spread + 1e-05) * gain + shift


def activate(values):
    return jax.nn.gelu(values, approximate=True)


def outer_sum(left, right):
    return jnp.einsum("rd,re->de", left, right, preferred_element_type=jnp.float32)


def column_sum(values):
    return jnp.sum(values.astype(jnp.float32), axis=0)


def masked_scores(queries, key_heads, query_ids, key_ids):
    score_scale = queries.shape[-1] ** (-0.5)
    score = (
        jnp.einsum("qhd,khd->hqk", queries, key_heads, preferred_element_type=jnp.float32)
        * score_scale
    )
    same_doc = query_ids[None, :, None] == key_ids[None, None, :]
    return jnp.where(same_doc, score, -1e30)


def forward_one(seq_item):
    queries, key_heads, value_heads, query_ids, key_ids = seq_item
    score = masked_scores(queries, key_heads, query_ids, key_ids)
    row_max = jnp.max(score, axis=-1, keepdims=True)
    log_total = row_max + jnp.log(jnp.sum(jnp.exp(score - row_max), axis=-1, keepdims=True))
    weights = jnp.exp(score - log_total).astype(jnp.bfloat16)
    attended = jnp.einsum("hqk,khd->qhd", weights, value_heads, preferred_element_type=jnp.float32)
    return (attended.astype(jnp.bfloat16), log_total)


def backward_one(seq_item):
    queries, key_heads, value_heads, query_ids, key_ids, log_total, d_attended = seq_item
    score_scale = queries.shape[-1] ** (-0.5)
    score = masked_scores(queries, key_heads, query_ids, key_ids)
    probs = jnp.exp(score - log_total)
    d_probs = jnp.einsum(
        "qhd,khd->hqk", d_attended, value_heads, preferred_element_type=jnp.float32
    )
    inner = jnp.sum(probs * d_probs, axis=-1, keepdims=True)
    d_score = (probs * (d_probs - inner)).astype(jnp.bfloat16)
    d_query = (
        jnp.einsum("hqk,khd->qhd", d_score, key_heads, preferred_element_type=jnp.float32)
        * score_scale
    )
    d_key = (
        jnp.einsum("hqk,qhd->khd", d_score, queries, preferred_element_type=jnp.float32)
        * score_scale
    )
    d_value = jnp.einsum(
        "hqk,qhd->khd", probs.astype(jnp.bfloat16), d_attended, preferred_element_type=jnp.float32
    )
    return (d_query, d_key, d_value)


def shards(
    hidden_in,
    segment_ids,
    teacher,
    w_query,
    b_query,
    w_key,
    w_value,
    b_value,
    w_output,
    b_output,
    first_gain,
    first_shift,
    w_inner,
    b_inner,
    w_outer,
    b_outer,
    second_gain,
    second_shift,
):
    seq_count, span_len, model_width = hidden_in.shape
    row_count = seq_count * span_len
    local_width = w_query.shape[1]
    head_count = local_width // HD
    inputs = hidden_in.reshape(row_count, model_width)
    queries = (jnp.dot(inputs, w_query, preferred_element_type=jnp.float32) + b_query).astype(
        jnp.bfloat16
    )
    key_rows = jnp.dot(inputs, w_key, preferred_element_type=jnp.float32).astype(jnp.bfloat16)
    value_rows = (jnp.dot(inputs, w_value, preferred_element_type=jnp.float32) + b_value).astype(
        jnp.bfloat16
    )
    key_local = key_rows.reshape(seq_count, span_len, local_width)
    value_local = value_rows.reshape(seq_count, span_len, local_width)

    def heads_view(block_in):
        return block_in.reshape(block_in.shape[0], block_in.shape[1], head_count, HD)

    gathered = (
        lax.all_gather(key_local, "ctx", axis=1, tiled=True),
        lax.all_gather(value_local, "ctx", axis=1, tiled=True),
        lax.all_gather(segment_ids, "ctx", axis=1, tiled=True),
    )
    query_heads = heads_view(queries.reshape(seq_count, span_len, local_width))
    attended, log_total = lax.map(
        forward_one,
        (query_heads, heads_view(gathered[0]), heads_view(gathered[1]), segment_ids, gathered[2]),
    )
    attn_rows = attended.reshape(row_count, local_width)
    mixed_sum = (
        lax.psum(jnp.dot(attn_rows, w_output, preferred_element_type=jnp.float32), "tensor")
        + b_output
    )
    first_sum = inputs.astype(jnp.float32) + mixed_sum
    normed, first_back = jax.vjp(layer_norm, first_sum, first_gain, first_shift)
    normed_low = normed.astype(jnp.bfloat16)
    pre_act = jnp.dot(normed_low, w_inner, preferred_element_type=jnp.float32) + b_inner
    hidden_act, gelu_back = jax.vjp(activate, pre_act)
    act_low = hidden_act.astype(jnp.bfloat16)
    outer_part = (
        lax.psum(jnp.dot(act_low, w_outer, preferred_element_type=jnp.float32), "tensor") + b_outer
    )
    result, second_back = jax.vjp(layer_norm, normed + outer_part, second_gain, second_shift)
    valid_rows = (segment_ids.reshape(row_count) > 0).astype(jnp.float32)
    error_gap = result - teacher.reshape(row_count, model_width).astype(jnp.float32)
    error_sum, total_count = lax.psum(
        (jnp.sum(valid_rows[:, None] * error_gap * error_gap), jnp.sum(valid_rows)), ("dp", "ctx")
    )
    loss = error_sum / total_count
    token_slots = row_count * lax.axis_size("dp") * lax.axis_size("ctx")
    d_result = 2.0 * token_slots / total_count * valid_rows[:, None] * error_gap
    d_second, grad_second_gain, grad_second_shift = second_back(d_result)
    d_outer_low = d_second.astype(jnp.bfloat16)
    grad_b_outer = column_sum(d_outer_low)
    grad_w_outer = outer_sum(act_low, d_outer_low)
    d_act = jnp.dot(d_outer_low, w_outer.T, preferred_element_type=jnp.float32)
    d_pre_low = gelu_back(d_act)[0].astype(jnp.bfloat16)
    grad_b_inner = column_sum(d_pre_low)
    grad_w_inner = outer_sum(normed_low, d_pre_low)
    d_normed = d_second + lax.psum(
        jnp.dot(d_pre_low, w_inner.T, preferred_element_type=jnp.float32), "tensor"
    )
    d_first, grad_first_gain, grad_first_shift = first_back(d_normed)
    d_mixed_low = d_first.astype(jnp.bfloat16)
    grad_b_output = column_sum(d_mixed_low)
    grad_w_output = outer_sum(attn_rows, d_mixed_low)
    d_attended = jnp.dot(d_mixed_low, w_output.T, preferred_element_type=jnp.float32).astype(
        jnp.bfloat16
    )
    d_attended_heads = heads_view(d_attended.reshape(seq_count, span_len, local_width))
    gathered = (
        lax.all_gather(key_local, "ctx", axis=1, tiled=True),
        lax.all_gather(value_local, "ctx", axis=1, tiled=True),
        lax.all_gather(segment_ids, "ctx", axis=1, tiled=True),
    )
    d_query, d_key_all, d_value_all = lax.map(
        backward_one,
        (
            query_heads,
            heads_view(gathered[0]),
            heads_view(gathered[1]),
            segment_ids,
            gathered[2],
            log_total,
            d_attended_heads,
        ),
    )
    d_key_part, d_value_part = (
        lax.psum_scatter(d_key_all, "ctx", scatter_dimension=1, tiled=True),
        lax.psum_scatter(d_value_all, "ctx", scatter_dimension=1, tiled=True),
    )
    d_query_low = d_query.reshape(row_count, local_width).astype(jnp.bfloat16)
    d_key_low = d_key_part.reshape(row_count, local_width).astype(jnp.bfloat16)
    d_value_low = d_value_part.reshape(row_count, local_width).astype(jnp.bfloat16)
    grad_b_query = column_sum(d_query_low)
    grad_b_value = column_sum(d_value_low)
    grad_w_query = outer_sum(inputs, d_query_low)
    grad_w_key = outer_sum(inputs, d_key_low)
    grad_w_value = outer_sum(inputs, d_value_low)
    back_in = jnp.dot(d_query_low, w_query.T, preferred_element_type=jnp.float32)
    back_in = back_in + jnp.dot(d_key_low, w_key.T, preferred_element_type=jnp.float32)
    back_in = back_in + jnp.dot(d_value_low, w_value.T, preferred_element_type=jnp.float32)
    grad_input = d_first + lax.psum(back_in, "tensor")
    grad_w_query, grad_w_key, grad_w_value, grad_w_output, grad_w_inner, grad_w_outer = (
        lax.psum_scatter(grad_w_query, ("dp", "ctx"), scatter_dimension=0, tiled=True),
        lax.psum_scatter(grad_w_key, ("dp", "ctx"), scatter_dimension=0, tiled=True),
        lax.psum_scatter(grad_w_value, ("dp", "ctx"), scatter_dimension=0, tiled=True),
        lax.psum_scatter(grad_w_output, ("dp", "ctx"), scatter_dimension=1, tiled=True),
        lax.psum_scatter(grad_w_inner, ("dp", "ctx"), scatter_dimension=0, tiled=True),
        lax.psum_scatter(grad_w_outer, ("dp", "ctx"), scatter_dimension=1, tiled=True),
    )
    (
        grad_b_query,
        grad_b_value,
        grad_b_output,
        grad_first_gain,
        grad_first_shift,
        grad_b_inner,
        grad_b_outer,
        grad_second_gain,
        grad_second_shift,
    ) = (
        lax.psum(grad_b_query.astype(jnp.bfloat16), ("dp", "ctx")).astype(jnp.float32),
        lax.psum(grad_b_value.astype(jnp.bfloat16), ("dp", "ctx")).astype(jnp.float32),
        lax.psum(grad_b_output.astype(jnp.bfloat16), ("dp", "ctx")).astype(jnp.float32),
        lax.psum(grad_first_gain.astype(jnp.bfloat16), ("dp", "ctx")).astype(jnp.float32),
        lax.psum(grad_first_shift.astype(jnp.bfloat16), ("dp", "ctx")).astype(jnp.float32),
        lax.psum(grad_b_inner.astype(jnp.bfloat16), ("dp", "ctx")).astype(jnp.float32),
        lax.psum(grad_b_outer.astype(jnp.bfloat16), ("dp", "ctx")).astype(jnp.float32),
        lax.psum(grad_second_gain.astype(jnp.bfloat16), ("dp", "ctx")).astype(jnp.float32),
        lax.psum(grad_second_shift.astype(jnp.bfloat16), ("dp", "ctx")).astype(jnp.float32),
    )
    layer_out = result.astype(jnp.bfloat16).reshape(seq_count, span_len, model_width)
    return (
        layer_out,
        loss,
        grad_input.reshape(seq_count, span_len, model_width),
        grad_w_query,
        grad_b_query,
        grad_w_key,
        grad_w_value,
        grad_b_value,
        grad_w_output,
        grad_b_output,
        grad_first_gain,
        grad_first_shift,
        grad_w_inner,
        grad_b_inner,
        grad_w_outer,
        grad_b_outer,
        grad_second_gain,
        grad_second_shift,
    )


def solution(mesh):
    placed = (
        P("dp", "ctx", None),
        P("dp", "ctx"),
        P("dp", "ctx", None),
        P(None, "tensor"),
        P("tensor"),
        P(None, "tensor"),
        P(None, "tensor"),
        P("tensor"),
        P("tensor", None),
        P(),
        P(),
        P(),
        P(None, "tensor"),
        P("tensor"),
        P("tensor", None),
        P(),
        P(),
        P(),
    )
    return jax.shard_map(
        shards,
        mesh=mesh,
        in_specs=placed,
        out_specs=(
            P("dp", "ctx", None),
            P(),
            P("dp", "ctx", None),
            P(("dp", "ctx"), "tensor"),
            P("tensor"),
            P(("dp", "ctx"), "tensor"),
            P(("dp", "ctx"), "tensor"),
            P("tensor"),
            P("tensor", ("dp", "ctx")),
            P(),
            P(),
            P(),
            P(("dp", "ctx"), "tensor"),
            P("tensor"),
            P("tensor", ("dp", "ctx")),
            P(),
            P(),
            P(),
        ),
        check_vma=False,
    )
```

profile of v0, /device:TPU:0, one launch (start us, length us, event | category | flops | bytes accessed | tf_op | source)
XLA Modules:
  0.0 1397.7 jit_solution(5472246743075530100)
XLA Ops:
  7.3 3.6 convolution_convert_fusion.1
  12.0 3.5 fusion.58
  16.6 3.5 fusion.59
  20.3 9.5 all_gather.13
  29.8 20.2 %all-gather.5.cloned.1.call-done = bf16[2,1024,512]{1,2,0:T(8,128)(2,1)} async-done(((bf16[2,256,512]{1,2,0:T(8,128)(2,1)}), bf16[2,1024,512]{1,2,0:T(8,128)(2,1)}) %all-gather.5.cloned.1.call-update) | async-done | bytes 2097168 | tf_op jit(solution)/shard_map/all_gather | solution.py:110
  50.0 3.9 copy.52
  53.9 33.7 %all-gather.3.cloned.1.call-done = bf16[2,1024,512]{1,2,0:T(8,128)(2,1)} async-done(((bf16[2,256,512]{1,2,0:T(8,128)(2,1)}), bf16[2,1024,512]{1,2,0:T(8,128)(2,1)}) %all-gather.3.cloned.1.call-update) | async-done | bytes 2097168 | tf_op jit(solution)/shard_map/all_gather | solution.py:111
  87.6 12.4 while.26
  87.9 2.4 fusion.137
  94.0 2.4 fusion.137
  100.0 4.3 fusion.70
  104.6 154.9 %all-reduce.6.cloned.1.call-done = f32[512,2048]{1,0:T(8,128)} async-done(((f32[512,2048]{1,0:T(8,128)}), f32[512,2048]{1,0:T(8,128)}) %all-reduce.6.cloned.1.call-update) | async-done | bytes 4194320 | tf_op jit(solution)/shard_map/psum | solution.py:121
  259.5 3.5 fusion.96
  263.8 8.9 fusion.86
  272.7 2.0 copy-done.35
  274.7 7.0 fusion.83
  282.4 15.6 %psum.108 = f32[]{:T(128)} all-reduce(f32[]{:T(128)} %convert_reduce_fusion), channel_id=1, replica_groups=mesh['dp'=2,'ctx'=4,'tensor'=4] {'dp','ctx'}, use_global_device_ids=true, to_apply=%region_13.14 | all-reduce | flops 1 | bytes 8 | tf_op jit(solution)/shard_map/psum | solution.py:136
  298.7 137.2 %all-reduce.8.cloned.1.call-done = f32[512,2048]{1,0:T(8,128)} async-done(((f32[512,2048]{1,0:T(8,128)}), f32[512,2048]{1,0:T(8,128)}) %all-reduce.8.cloned.1.call-update) | async-done | bytes 4194320 | tf_op jit(solution)/shard_map/psum | solution.py:131
  435.9 4.7 fusion.95
  442.2 4.2 multiply_reduce_fusion.7
  446.4 3.4 fusion.94
  449.9 2.0 copy-done.5
  452.9 9.6 fusion.89
  462.4 1.3 copy-done.36
  463.8 9.6 fusion.97
  474.0 153.6 %all-reduce.10.cloned.1.call-done = f32[512,2048]{1,0:T(8,128)} async-done(((f32[512,2048]{1,0:T(8,128)}), f32[512,2048]{1,0:T(8,128)}) %all-reduce.10.cloned.1.call-update) | async-done | bytes 4194320 | tf_op jit(solution)/shard_map/psum | solution.py:150
  627.6 6.0 multiply_reduce_fusion.2
  634.8 1.9 copy-done.6
  638.5 2.1 convolution_convert_fusion
  641.7 23.1 %while.27 = (s32[]{:T(128)}, bf16[2,256,4,128]{1,3,2,0:T(8,128)(2,1)S(1)}, f32[2,1024,4,128]{1,3,2,0:T(8,128)}, f32[2,1024,4,128]{1,3,2,0:T(8,128)}, bf16[2,1024...) while((s32[]{:T(128)}, ...), condition=%wide.region_21.22_spmd, body=%wide.region_19.21_spmd.sunk | while | flops 1358822400 | bytes 92322544 | solution.py:166
  642.0 2.1 fusion.146
  644.2 1.7 multiply_reduce_fusion.9
  650.6 2.7 bitcast_dynamic-update-slice_fusion.8
  653.6 2.1 fusion.146
  655.8 1.7 multiply_reduce_fusion.9
  662.2 2.6 bitcast_dynamic-update-slice_fusion.8
  666.6 3.2 convolution_bitcast_fusion.2
  670.1 5.2 fusion.66
  675.3 41.4 %reduce-scatter.9.cloned.1.call-done = f32[2,256,4,128]{1,3,2,0:T(8,128)} async-done(((f32[2,1024,4,128]{1,3,2,0:T(8,128)}), f32[2,256,4,128]{1,3,2,0:T(8,128)}) %reduce-scatter.9.cloned.1.call-update) | async-done | bytes 1048592 | tf_op jit(solution)/shard_map/reduce_scatter | solution.py:179
  718.3 54.1 %reduce-scatter.11.cloned.1.call-done = f32[2,256,4,128]{1,3,2,0:T(8,128)} async-done(((f32[2,1024,4,128]{1,3,2,0:T(8,128)}), f32[2,256,4,128]{1,3,2,0:T(8,128)}) %reduce-scatter.11.cloned.1.call-update) | async-done | bytes 1048592 | tf_op jit(solution)/shard_map/reduce_scatter | solution.py:180
  772.4 2.1 fusion.92
  774.5 1.3 copy.60
  775.8 3.0 fusion.63
  779.3 3.3 add_add_fusion.2
  782.7 3.2 convolution_bitcast_fusion
  786.0 3.3 convolution_bitcast_fusion.1
  789.4 1.6 copy-done.12
  791.0 3.2 fusion.68
  794.3 1.5 copy-done.37
  795.8 10.7 fusion.84
  806.7 1.3 copy-done.17
  808.0 11.8 fusion.82
  819.9 14.9 %psum.107 = f32[]{:T(128)} all-reduce(f32[]{:T(128)} %get-tuple-element.204), channel_id=1, replica_groups=mesh['dp'=2,'ctx'=4,'tensor'=4] {'dp','ctx'}, use_global_device_ids=true, to_apply=%region_11.12 | all-reduce | flops 1 | bytes 8 | tf_op jit(solution)/shard_map/psum | solution.py:136
  836.4 2.1 copy.61
  838.5 26.8 %all-reduce = (bf16[512]{0:T(512)(128)(2,1)S(1)}, bf16[512]{0:T(512)(128)(2,1)S(1)}, bf16[2048]{0:T(1024)(128)(2,1)S(1)}, bf16[2048]{0:T(1024)(128)(2,1)S(1)}, b...) all-reduce(bf16[512]{0:T(512)(128)(2,1)S(1)} %bitcast.223, ...), channel_id=1, replica_groups=mesh['dp'=2,'ctx'=4,'tensor'=4] {'dp','ctx'}, use_global_device_ids=true, to_apply=%region_27.28 | all-reduce | flops 15360 | bytes 61440 | tf_op jit(solution)/shard_map/psum | solution.py:213
  870.6 114.9 %all-reduce.12.cloned.1.call-done = f32[512,2048]{1,0:T(8,128)} async-done(((f32[512,2048]{1,0:T(8,128)}), f32[512,2048]{1,0:T(8,128)}) %all-reduce.12.cloned.1.call-update) | async-done | bytes 4194320 | tf_op jit(solution)/shard_map/psum | solution.py:193
  985.5 6.1 add_add_fusion.5
  991.6 47.8 %reduce-scatter.17.cloned.1.call-done = f32[256,512]{0,1:T(8,128)} async-done(((f32[2048,512]{0,1:T(8,128)}), f32[256,512]{0,1:T(8,128)}) %reduce-scatter.17.cloned.1.call-update) | async-done | bytes 524304 | tf_op jit(solution)/shard_map/reduce_scatter | solution.py:197
  1039.5 2.0 copy.63
  1041.5 52.7 %reduce-scatter.15.cloned.1.call-done = f32[256,512]{0,1:T(8,128)} async-done(((f32[2048,512]{0,1:T(8,128)}), f32[256,512]{0,1:T(8,128)}) %reduce-scatter.15.cloned.1.call-update) | async-done | bytes 524304 | tf_op jit(solution)/shard_map/reduce_scatter | solution.py:196
  1094.1 2.0 copy.62
  1096.2 53.5 %reduce-scatter.19.cloned.1.call-done = f32[512,256]{1,0:T(8,128)} async-done(((f32[512,2048]{1,0:T(8,128)}), f32[512,256]{1,0:T(8,128)}) %reduce-scatter.19.cloned.1.call-update) | async-done | bytes 524304 | tf_op jit(solution)/shard_map/reduce_scatter | solution.py:198
  1149.7 120.1 %reduce-scatter.21.cloned.1.call-done = f32[256,2048]{1,0:T(8,128)} async-done(((f32[2048,2048]{1,0:T(8,128)}), f32[256,2048]{1,0:T(8,128)}) %reduce-scatter.21.cloned.1.call-update) | async-done | bytes 2097168 | tf_op jit(solution)/shard_map/reduce_scatter | solution.py:199
  1269.8 120.0 %reduce-scatter.23.cloned.1.call-done = f32[2048,256]{1,0:T(8,128)} async-done(((f32[2048,2048]{1,0:T(8,128)}), f32[2048,256]{1,0:T(8,128)}) %reduce-scatter.23.cloned.1.call-update) | async-done | bytes 2097168 | tf_op jit(solution)/shard_map/reduce_scatter | solution.py:200
  (191 shorter events, 39.0 us)
Async XLA Ops:
  7.2 92.8 %copy-start = (bf16[512,2048]{1,0:T(8,128)(2,1)S(1)}, bf16[512,2048]{1,0:T(8,128)(2,1)}, u32[]{:S(2)}) copy-start(bf16[512,2048]{1,0:T(8,128)(2,1)} %param.30) | copy-start | bytes 6291460
  7.2 42.8 %all-gather.5.cloned.1.call-start = ((), (), s32[]{:S(2)}) async-start(), calls=%async_computation.9 | async-start | bytes 2621440 | tf_op jit(solution)/shard_map/all_gather | solution.py:110
  7.3 4.7 copy-start.33
  11.9 4.6 copy-start.34
  11.9 75.7 %all-gather.3.cloned.1.call-start = ((), (), s32[]{:S(2)}) async-start(), calls=%async_computation.8 | async-start | bytes 2621440 | tf_op jit(solution)/shard_map/all_gather | solution.py:111
  16.5 243.0 %all-reduce.6.cloned.1.call-start = ((), (), s32[]{:S(2)}) async-start(), calls=%async_computation.10 | async-start | bytes 8388608 | tf_op jit(solution)/shard_map/psum | solution.py:121
  16.6 3.7 copy-start.22
  87.8 3.6 copy-start.9
  94.0 3.6 copy-start.9
  100.0 159.5 %copy-start.29 = (f32[2048]{0:T(1024)S(1)}, f32[2048]{0:T(1024)}, u32[]{:S(2)}) copy-start(f32[2048]{0:T(1024)} %param.31) | copy-start | bytes 24580
  104.3 331.6 %all-reduce.8.cloned.1.call-start = ((), (), s32[]{:S(2)}) async-start(), calls=%async_computation.11 | async-start | bytes 8388608 | tf_op jit(solution)/shard_map/psum | solution.py:131
  263.0 9.7 copy-start.3
  263.0 0.7 copy-start.23
  263.0 0.8 copy-start.31
  263.0 11.7 slice-start
  263.7 11.0 slice-start.1
  263.7 11.0 copy-start.32
  272.7 2.0 copy-start.35
  281.7 154.2 %copy-start.30 = (f32[2048]{0:T(1024)S(1)}, f32[2048]{0:T(1024)}, u32[]{:S(2)}) copy-start(f32[2048]{0:T(1024)} %param.37) | copy-start | bytes 24580
  281.7 345.9 %all-reduce.10.cloned.1.call-start = ((), (), s32[]{:S(2)}) async-start(), calls=%async_computation.12 | async-start | bytes 8388608 | tf_op jit(solution)/shard_map/psum | solution.py:150
  440.6 1.6 copy-start.13
  440.6 1.6 copy-start.24
  440.6 1.6 copy-start.25
  446.4 6.5 slice-start.2
  446.4 6.5 slice-start.3
  449.9 2.0 copy-start.5
  452.9 9.6 copy-start.16
  462.4 1.3 copy-start.36
  473.4 243.3 %reduce-scatter.9.cloned.1.call-start = ((), (), s32[]{:S(2)}) async-start(), calls=%async_computation.13 | async-start | bytes 5242880 | tf_op jit(solution)/shard_map/reduce_scatter | solution.py:179
  627.6 6.0 copy-start.4
  634.8 2.0 copy-start.6
  637.2 1.3 copy-start.11
  641.7 2.5 copy-start.10
  645.9 2.2 copy-start.14
  647.2 1.8 copy-start.2
  648.6 2.0 copy-start.15
  653.4 2.4 copy-start.10
  657.5 2.2 copy-start.14
  658.8 1.8 copy-start.2
  660.2 2.0 copy-start.15
  664.8 0.8 copy-start.18
  664.9 1.8 copy-start.7
  664.9 107.5 %reduce-scatter.11.cloned.1.call-start = ((), (), s32[]{:S(2)}) async-start(), calls=%async_computation.14 | async-start | bytes 5242880 | tf_op jit(solution)/shard_map/reduce_scatter | solution.py:180
  665.6 170.7 %reduce-scatter.13.cloned.1.call-start = ((), (), s32[]{:S(2)}) async-start(), calls=%async_computation.16 | async-start | bytes 4718592 | tf_op jit(solution)/shard_map/reduce_scatter | solution.py:195
  669.9 315.7 %all-reduce.12.cloned.1.call-start = ((), (), s32[]{:S(2)}) async-start(), calls=%async_computation.15 | async-start | bytes 8388608 | tf_op jit(solution)/shard_map/psum | solution.py:193
  775.8 3.1 copy-start.8
  775.8 3.5 copy-start.20
  782.6 256.8 %reduce-scatter.17.cloned.1.call-start = ((), (), s32[]{:S(2)}) async-start(), calls=%async_computation.18 | async-start | bytes 4718592 | tf_op jit(solution)/shard_map/reduce_scatter | solution.py:197
  785.9 3.5 copy-start.21
  785.9 308.2 %reduce-scatter.15.cloned.1.call-start = ((), (), s32[]{:S(2)}) async-start(), calls=%async_computation.17 | async-start | bytes 4718592 | tf_op jit(solution)/shard_map/reduce_scatter | solution.py:196
  789.3 1.7 copy-start.12
  789.3 360.3 %reduce-scatter.19.cloned.1.call-start = ((), (), s32[]{:S(2)}) async-start(), calls=%async_computation.19 | async-start | bytes 4718592 | tf_op jit(solution)/shard_map/reduce_scatter | solution.py:198
  794.2 1.6 copy-start.37
  794.2 475.6 %reduce-scatter.21.cloned.1.call-start = ((), (), s32[]{:S(2)}) async-start(), calls=%async_computation.20 | async-start | bytes 18874368 | tf_op jit(solution)/shard_map/reduce_scatter | solution.py:199
  806.4 1.6 copy-start.17
  806.5 583.3 %reduce-scatter.23.cloned.1.call-start = ((), (), s32[]{:S(2)}) async-start(), calls=%async_computation.21 | async-start | bytes 18874368 | tf_op jit(solution)/shard_map/reduce_scatter | solution.py:200
  819.9 16.3 %copy-start.19 = (bf16[2,256,4,128]{1,3,2,0:T(8,128)(2,1)S(1)}, bf16[2,256,4,128]{1,3,2,0:T(8,128)(2,1)}, u32[]{:S(2)}) copy-start(bf16[2,256,4,128]{1,3,2,0:T(8,128)(2,1)} %copy-done.18) | copy-start | bytes 1572868
  819.9 18.6 %copy-start.26 = (bf16[2048]{0:T(1024)(128)(2,1)S(1)}, bf16[2048]{0:T(1024)(128)(2,1)}, u32[]{:S(2)}) copy-start(bf16[2048]{0:T(1024)(128)(2,1)} %get-tuple-element.201) | copy-start | bytes 12292
  819.9 18.6 %copy-start.27 = (bf16[2048]{0:T(1024)(128)(2,1)S(1)}, bf16[2048]{0:T(1024)(128)(2,1)}, u32[]{:S(2)}) copy-start(bf16[2048]{0:T(1024)(128)(2,1)} %get-tuple-element.203) | copy-start | bytes 12292
  819.9 18.6 %copy-start.28 = (bf16[2048]{0:T(1024)(128)(2,1)S(1)}, bf16[2048]{0:T(1024)(128)(2,1)}, u32[]{:S(2)}) copy-start(bf16[2048]{0:T(1024)(128)(2,1)} %get-tuple-element.255) | copy-start | bytes 12292
  985.5 404.2 %copy-start.1 = (bf16[512,2048]{1,0:T(8,128)(2,1)S(1)}, bf16[512,2048]{1,0:T(8,128)(2,1)}, u32[]{:S(2)}) copy-start(bf16[512,2048]{1,0:T(8,128)(2,1)} %param.30) | copy-start | bytes 6291460
Sparse Core Ops, SparseCore 0:
  12.0 37.9 all-gather.4
  52.4 35.1 all-gather.2
  104.4 154.9 all-reduce.5
  281.8 153.9 all-reduce.7
  473.6 153.9 all-reduce.9
  665.0 51.6 reduce-scatter.8
  719.7 52.6 reduce-scatter.10
  776.1 51.3 reduce-scatter.12
  830.5 154.9 all-reduce.11
  989.1 50.3 reduce-scatter.16
  1042.8 51.2 reduce-scatter.14
  1098.3 51.3 reduce-scatter.18
  1153.8 115.9 reduce-scatter.20
  1273.8 115.9 reduce-scatter.22
where the time goes:
time: 1400 us
  waiting for transfers between devices  1100 us (79%)
  matrix products  122 us (9%)
  blocking collectives  66.9 us (5%)
  other arithmetic  47.2 us (3%)
  local copies, waits for them, and re-layouts  37.1 us (3%)
  between operations  17.8 us (1%)
    psum x1, waiting for transfers between devices, shards(): lax.psum(jnp.dot(attn_rows, w_output, preferred_element_type=jnp.float32)...  155 us
    psum x1, waiting for transfers between devices, shards(): lax.psum(jnp.dot(d_pre_low, w_inner.T, preferred_element_type=jnp.float32...  154 us
    psum x1, waiting for transfers between devices, shards(): lax.psum(jnp.dot(act_low, w_outer, preferred_element_type=jnp.float32), '...  137 us
    reduce_scatter x1, waiting for transfers between devices, shards(): lax.psum_scatter(grad_w_inner, ('dp', 'ctx'), scatter_dimension=0, tiled=...  120 us
    reduce_scatter x1, waiting for transfers between devices, shards(): lax.psum_scatter(grad_w_outer, ('dp', 'ctx'), scatter_dimension=1, tiled=...  120 us
    psum x1, waiting for transfers between devices, shards(): grad_input = d_first + lax.psum(back_in, 'tensor')  115 us
    reduce_scatter x1, waiting for transfers between devices, shards(): lax.psum_scatter(d_value_all, 'ctx', scatter_dimension=1, tiled=True)  54.1 us
    reduce_scatter x1, waiting for transfers between devices, shards(): lax.psum_scatter(grad_w_output, ('dp', 'ctx'), scatter_dimension=1, tiled...  53.5 us
  transfers between devices with their start and end apart: 14, of which 13 were waited for; matrix products, arithmetic and copies ran while one was open for 6% of the time, Pallas kernels for 0%

commit v1 on v0

--- a/solution.py
+++ b/solution.py
@@ -1,9 +1,13 @@
 import jax
 import jax.numpy as jnp
 from jax import lax
+from jax.experimental import pallas as pl
+from jax.experimental.pallas import tpu as pltpu
 from jax.sharding import PartitionSpec as P
 
 HD = 128
+VMEM_BYTES = 63 * 2**20
+GELU_A = 0.7978845608028654
 
 
 def layer_norm(values, gain, shift):
@@ -243,6 +247,1241 @@
     )
 
 
+MESH = pl.DeviceIdType.MESH
+F32 = jnp.float32
+BF16 = jnp.bfloat16
+CHUNKS = 8
+
+
+def place():
+    return lax.axis_index("dp"), lax.axis_index("ctx"), lax.axis_index("tensor")
+
+
+def dot(left, right):
+    return lax.dot_general(left, right, (((1,), (0,)), ((), ())), preferred_element_type=F32)
+
+
+def dot_nt(left, right):
+    return lax.dot_general(left, right, (((1,), (1,)), ((), ())), preferred_element_type=F32)
+
+
+def dot_tn(left, right):
+    return lax.dot_general(left, right, (((0,), (0,)), ((), ())), preferred_element_type=F32)
+
+
+def remote(src, dst, send, recv, device):
+    return pltpu.make_async_remote_copy(
+        src_ref=src,
+        dst_ref=dst,
+        send_sem=send,
+        recv_sem=recv,
+        device_id=device,
+        device_id_type=MESH,
+    )
+
+
+def greet(always, line):
+    d, c, t = place()
+    barrier = pltpu.get_barrier_semaphore()
+    for device in always:
+        pl.semaphore_signal(barrier, inc=1, device_id=device, device_id_type=MESH)
+    if line:
+        last = lax.axis_size("tensor") - 1
+
+        @pl.when(t < last)
+        def _():
+            pl.semaphore_signal(
+                barrier, inc=1, device_id=(d, c, jnp.minimum(t + 1, last)), device_id_type=MESH
+            )
+
+        @pl.when(t > 0)
+        def _():
+            pl.semaphore_signal(
+                barrier, inc=1, device_id=(d, c, jnp.maximum(t - 1, 0)), device_id_type=MESH
+            )
+
+    expected = len(always)
+    if line:
+        expected = expected + (t < last).astype(jnp.int32) + (t > 0).astype(jnp.int32)
+    pl.semaphore_wait(barrier, expected)
+
+
+def ctx_peers():
+    d, c, t = place()
+    return [(d, 3 - c, t), (d, c + 1 - 2 * lax.rem(c, 2), t), (d, lax.rem(c + 2, 4), t)]
+
+
+def line_sum(produce, line, beside=()):
+    sent, got, middle_got, total = line[:4]
+    end_send, end_recv, red_send, red_recv, out_send, out_recv, back_send, back_recv = line[4:]
+    d, c, t = place()
+    is_end = (t == 0) | (t == 3)
+    near = (t >= 2).astype(jnp.int32)
+    far = 1 - near
+    partner = (d, c, t + 1 - 2 * lax.rem(t, 2))
+    across = (d, c, 3 - t)
+
+    def end_copy(half, chunk):
+        return remote(
+            sent.at[half, chunk],
+            got.at[half, chunk],
+            end_send.at[half, chunk],
+            end_recv.at[half, chunk],
+            partner,
+        )
+
+    def reduce_copy(chunk):
+        return remote(
+            sent.at[far, chunk], middle_got.at[chunk], red_send.at[chunk], red_recv.at[chunk], across
+        )
+
+    def out_copy(half, chunk):
+        return remote(
+            total.at[half, chunk],
+            total.at[half, chunk],
+            out_send.at[half, chunk],
+            out_recv.at[half, chunk],
+            across,
+        )
+
+    def back_copy(half, chunk):
+        return remote(
+            total.at[half, chunk],
+            total.at[half, chunk],
+            back_send.at[half, chunk],
+            back_recv.at[half, chunk],
+            partner,
+        )
+
+    def inside(chunk):
+        return (chunk >= 0) & (chunk < CHUNKS)
+
+    def step(s, carry):
+        @pl.when(is_end & inside(s))
+        def _():
+            for half in (far, near):
+                sent[half, s] = produce(half, s).astype(BF16)
+                end_copy(half, s).start()
+
+        @pl.when(jnp.logical_not(is_end))
+        def _():
+            @pl.when(inside(s - 1))
+            def _():
+                chunk = s - 1
+                value = produce(far, chunk)
+                end_copy(far, chunk).wait_recv()
+                sent[far, chunk] = (value + got[far, chunk].astype(F32)).astype(BF16)
+                reduce_copy(chunk).start()
+
+            @pl.when(inside(s - 2))
+            def _():
+                chunk = s - 2
+                value = produce(near, chunk)
+                end_copy(near, chunk).wait_recv()
+                value = value + got[near, chunk].astype(F32)
+                reduce_copy(chunk).wait_recv()
+                total[near, chunk] = (value + middle_got[chunk].astype(F32)).astype(BF16)
+                out_copy(near, chunk).start()
+                back_copy(near, chunk).start()
+
+            @pl.when(inside(s - 3))
+            def _():
+                out_copy(far, s - 3).wait_recv()
+                back_copy(far, s - 3).start()
+
+        for at, task in beside:
+            pl.when(s == at)(task)
+        return carry
+
+    lax.fori_loop(0, CHUNKS + 3, step, 0)
+
+    def drain(chunk, carry):
+        @pl.when(is_end)
+        def _():
+            for half in (near, far):
+                back_copy(half, chunk).wait_recv()
+                end_copy(half, chunk).wait_send()
+
+        @pl.when(jnp.logical_not(is_end))
+        def _():
+            reduce_copy(chunk).wait_send()
+            out_copy(near, chunk).wait_send()
+            for half in (near, far):
+                back_copy(half, chunk).wait_send()
+
+        return carry
+
+    lax.fori_loop(0, CHUNKS, drain, 0)
+
+
+def line_scratch(rows, width):
+    half = rows // 2
+    columns = width // CHUNKS
+    block = pltpu.VMEM((2, CHUNKS, half, columns), BF16)
+    pair, single = pltpu.SemaphoreType.DMA((2, CHUNKS)), pltpu.SemaphoreType.DMA((CHUNKS,))
+    return [block, block, pltpu.VMEM((CHUNKS, half, columns), BF16), block] + [
+        pair, pair, single, single, pair, pair, pair, pair
+    ]
+
+
+LINE_REFS = 12
+
+
+STEP_ROWS = 32
+
+
+def row_block(total, step):
+    per_half = total.shape[2] // STEP_ROWS
+    half = step // per_half
+    start = pl.multiple_of((step - half * per_half) * STEP_ROWS, STEP_ROWS)
+    return jnp.concatenate(
+        [total[half, chunk, pl.ds(start, STEP_ROWS), :] for chunk in range(CHUNKS)], axis=1
+    ).astype(F32)
+
+
+def rows_at(step):
+    return pl.ds(pl.multiple_of(step * STEP_ROWS, STEP_ROWS), STEP_ROWS)
+
+
+def fold(values):
+    return jnp.sum(values.reshape(values.shape[0] // 8, 8, values.shape[1]), axis=0)
+
+
+def mean_last(values):
+    return jnp.mean(values, axis=-1, keepdims=True)
+
+
+def scatter_scratch(tiles, rows, columns):
+    return [
+        pltpu.VMEM((2, tiles, rows, columns), BF16),
+        pltpu.VMEM((4, tiles, rows, columns), BF16),
+        pltpu.VMEM((3, tiles, rows, columns), BF16),
+        pltpu.VMEM((3, tiles, rows, columns), BF16),
+        pltpu.SemaphoreType.DMA((4,)),
+        pltpu.SemaphoreType.DMA((4,)),
+        pltpu.SemaphoreType.DMA((3,)),
+        pltpu.SemaphoreType.DMA((3,)),
+    ]
+
+
+SCATTER_REFS = 8
+
+
+class Scatter:
+    def __init__(self, compute, read, write, refs):
+        self.compute, self.read, self.write = compute, read, write
+        self.core_out, self.core_in, self.cross_out, self.cross_in = refs[:4]
+        self.core_send, self.core_recv, self.cross_send, self.cross_recv = refs[4:]
+        self.tiles = self.core_in.shape[1]
+        d, c, t = place()
+        self.core = d
+        self.other = (1 - d, c, t)
+        self.peers = ctx_peers()
+        self.targets = [peer[1] for peer in self.peers] + [c]
+
+    def core_copy(self, unit):
+        return remote(
+            self.core_out.at[unit % 2],
+            self.core_in.at[unit],
+            self.core_send.at[unit],
+            self.core_recv.at[unit],
+            self.other,
+        )
+
+    def cross_copy(self, unit):
+        return remote(
+            self.cross_out.at[unit],
+            self.cross_in.at[unit],
+            self.cross_send.at[unit],
+            self.cross_recv.at[unit],
+            self.peers[unit],
+        )
+
+    def loop(self, body):
+        def step(tile, carry):
+            body(tile)
+            return carry
+
+        lax.fori_loop(0, self.tiles, step, 0)
+
+    def give(self, unit):
+        if unit >= 2:
+            self.core_copy(unit - 2).wait_send()
+
+        def body(tile):
+            value = self.compute(1 - self.core, self.targets[unit], tile)
+            self.core_out[unit % 2, tile] = value.astype(BF16)
+
+        self.loop(body)
+        self.core_copy(unit).start()
+
+    def take(self, unit):
+        self.core_copy(unit).wait_recv()
+
+        def body(tile):
+            value = self.compute(self.core, self.targets[unit], tile)
+            value = value + self.core_in[unit, tile].astype(F32)
+            if unit < 3:
+                self.cross_out[unit, tile] = value.astype(BF16)
+            else:
+                self.write(tile, value)
+
+        self.loop(body)
+        if unit < 3:
+            self.cross_copy(unit).start()
+
+    def finish(self):
+        for unit in range(3):
+            self.cross_copy(unit).wait_recv()
+
+        def body(tile):
+            value = self.read(tile)
+            for unit in range(3):
+                value = value + self.cross_in[unit, tile].astype(F32)
+            self.write(tile, value)
+
+        self.loop(body)
+        for unit in range(3):
+            self.cross_copy(unit).wait_send()
+        self.core_copy(2).wait_send()
+        self.core_copy(3).wait_send()
+
+    def pairs(self):
+        def both(unit):
+            def run():
+                if unit < 3:
+                    self.give(unit + 1)
+                self.take(unit)
+
+            return run
+
+        return [both(unit) for unit in range(4)]
+
+
+def tile_at(index, size):
+    return pl.ds(pl.multiple_of(index * size, size), size)
+
+
+def id_columns(row):
+    return jnp.broadcast_to(row, (128, row.shape[1])).T[:, :1]
+
+
+PIECES = 8
+
+
+class Line:
+    def __init__(self, refs, produce):
+        self.sent, self.got, self.middle_got, self.total = refs[:4]
+        (
+            self.end_send,
+            self.end_recv,
+            self.red_send,
+            self.red_recv,
+            self.out_send,
+            self.out_recv,
+            self.back_send,
+            self.back_recv,
+        ) = refs[4:]
+        self.produce = produce
+        d, c, t = place()
+        self.is_end = (t == 0) | (t == 3)
+        self.near = (t >= 2).astype(jnp.int32)
+        self.far = 1 - self.near
+        self.partner = (d, c, t + 1 - 2 * lax.rem(t, 2))
+        self.across = (d, c, 3 - t)
+
+    def end_copy(self, half, piece):
+        return remote(
+            self.sent.at[half, piece],
+            self.got.at[half, piece],
+            self.end_send.at[half, piece],
+            self.end_recv.at[half, piece],
+            self.partner,
+        )
+
+    def reduce_copy(self, piece):
+        return remote(
+            self.sent.at[self.far, piece],
+            self.middle_got.at[piece],
+            self.red_send.at[piece],
+            self.red_recv.at[piece],
+            self.across,
+        )
+
+    def out_copy(self, half, piece):
+        return remote(
+            self.total.at[half, piece],
+            self.total.at[half, piece],
+            self.out_send.at[half, piece],
+            self.out_recv.at[half, piece],
+            self.across,
+        )
+
+    def back_copy(self, half, piece):
+        return remote(
+            self.total.at[half, piece],
+            self.total.at[half, piece],
+            self.back_send.at[half, piece],
+            self.back_recv.at[half, piece],
+            self.partner,
+        )
+
+    def step(self, s):
+        near, far = self.near, self.far
+
+        def inside(piece):
+            return (piece >= 0) & (piece < PIECES)
+
+        @pl.when(self.is_end & inside(s))
+        def _():
+            for half in (far, near):
+                self.sent[half, s] = self.produce(half, s).astype(BF16)
+                self.end_copy(half, s).start()
+
+        @pl.when(jnp.logical_not(self.is_end))
+        def _():
+            @pl.when(inside(s - 1))
+            def _():
+                piece = s - 1
+                value = self.produce(far, piece)
+                self.end_copy(far, piece).wait_recv()
+                self.sent[far, piece] = (value + self.got[far, piece].astype(F32)).astype(BF16)
+                self.reduce_copy(piece).start()
+
+            @pl.when(inside(s - 2))
+            def _():
+                piece = s - 2
+                value = self.produce(near, piece)
+                self.end_copy(near, piece).wait_recv()
+                value = value + self.got[near, piece].astype(F32)
+                self.reduce_copy(piece).wait_recv()
+                value = value + self.middle_got[piece].astype(F32)
+                self.total[near, piece] = value.astype(BF16)
+                self.out_copy(near, piece).start()
+                self.back_copy(near, piece).start()
+
+            @pl.when(inside(s - 3))
+            def _():
+                self.out_copy(far, s - 3).wait_recv()
+                self.back_copy(far, s - 3).start()
+
+    def arrived(self):
+        @pl.when(self.is_end)
+        def _():
+            def body(piece, carry):
+                self.back_copy(self.near, piece).wait_recv()
+                self.back_copy(self.far, piece).wait_recv()
+                return carry
+
+            lax.fori_loop(0, PIECES, body, 0)
+
+    def drain(self):
+        def body(piece, carry):
+            @pl.when(self.is_end)
+            def _():
+                self.end_copy(self.near, piece).wait_send()
+                self.end_copy(self.far, piece).wait_send()
+
+            @pl.when(jnp.logical_not(self.is_end))
+            def _():
+                self.reduce_copy(piece).wait_send()
+                self.out_copy(self.near, piece).wait_send()
+                self.back_copy(self.near, piece).wait_send()
+                self.back_copy(self.far, piece).wait_send()
+
+            return carry
+
+        lax.fori_loop(0, PIECES, body, 0)
+
+    def rows(self, start):
+        return jnp.concatenate(
+            [
+                self.total[half, piece, pl.ds(start, STEP_ROWS), :]
+                for half in range(2)
+                for piece in range(PIECES)
+            ],
+            axis=1,
+        ).astype(F32)
+
+
+def stream_scratch(span, width):
+    columns = width // (2 * PIECES)
+    block = pltpu.VMEM((2, PIECES, span, columns), BF16)
+    pair, single = pltpu.SemaphoreType.DMA((2, PIECES)), pltpu.SemaphoreType.DMA((PIECES,))
+    return [block, block, pltpu.VMEM((PIECES, span, columns), BF16), block] + [
+        pair, pair, single, single, pair, pair, pair, pair
+    ]
+
+
+def run_stream(lines, tasks):
+    for k, line in enumerate(lines):
+
+        def step(j, carry, k=k, line=line):
+            if k > 0:
+                lines[k - 1].step(j + PIECES)
+            line.step(j)
+            for at, task in tasks[k]:
+                pl.when(j == at)(task)
+            return carry
+
+        lax.fori_loop(0, PIECES, step, 0)
+
+    def last(j, carry):
+        lines[-1].step(j + PIECES)
+        return carry
+
+    lax.fori_loop(0, 3, last, 0)
+
+
+def each_block(span, body):
+    def step(i, carry):
+        body(pl.multiple_of(i * STEP_ROWS, STEP_ROWS))
+        return carry
+
+    lax.fori_loop(0, span // STEP_ROWS, step, 0)
+
+
+def forward_kernel(
+    x_hbm, ids_ref, valid_ref, wq_hbm, wk_hbm, wv_hbm, bias_ref, wo_hbm, wi_hbm, bi_ref, wf_hbm, teacher_hbm, vec_ref,
+    all_ids_ref, qkv_hbm, lse_ref, o_hbm, low_hbm, out_hbm, dpre_hbm, dmix_hbm, sums_ref, bsum_ref, error_ref, gouter_hbm,
+    x_ref, wf_ref, wi_ref, wo_ref, qkv_ref, psend, o_ref, osend, norm_ref, rstd_ref, low_ref, act_ref, slope_ref, dlow_ref, mix_ref, gouter_ref,
+    lsem, wsem, pssem, prsem, isem, jsem, ossem, orsem, *refs,
+):
+    d, c, t = place()
+    span = ids_ref.shape[1]
+    local = wi_ref.shape[1]
+    width = x_ref.shape[1]
+    peers = ctx_peers()
+    targets = [peer[1] for peer in peers] + [c]
+    load_x = pltpu.make_async_copy(x_hbm, x_ref, lsem.at[0])
+    load_x.start()
+    loads = []
+    for k, head in enumerate(targets):
+        group = []
+        for i, w in enumerate((wq_hbm, wk_hbm, wv_hbm)):
+            at = (3 * k + i) * HD
+            load = pltpu.make_async_copy(
+                w.at[:, tile_at(head, HD)], wf_ref.at[:, at : at + HD], wsem.at[k, i]
+            )
+            load.start()
+            group.append(load)
+        loads.append(group)
+    load_wo = pltpu.make_async_copy(wo_hbm, wo_ref, lsem.at[1])
+    load_wo.start()
+    load_wi = pltpu.make_async_copy(wi_hbm, wi_ref, lsem.at[2])
+    load_wi.start()
+    load_teacher = pltpu.make_async_copy(teacher_hbm, mix_ref, lsem.at[3])
+    load_teacher.start()
+    load_wf = pltpu.make_async_copy(wf_hbm, wf_ref, lsem.at[4])
+    others = [(d, target, t) for target in targets[:3]] + [(1 - d, target, t) for target in targets]
+    greet(others, True)
+    all_ids_ref[d, c] = ids_ref[...]
+    id_copies = []
+    for i, other in enumerate(others):
+        copy = remote(ids_ref, all_ids_ref.at[d, c], isem.at[i], jsem.at[i], other)
+        copy.start()
+        id_copies.append(copy)
+    sums_ref[...] = jnp.zeros_like(sums_ref)
+    bsum_ref[...] = jnp.zeros_like(bsum_ref)
+    error_ref[...] = jnp.zeros_like(error_ref)
+    load_x.wait()
+
+    here = tile_at(c, span)
+
+    def project_copy(k, s):
+        return remote(
+            psend.at[k, s], qkv_ref.at[:, s, here, :], pssem.at[k, s], prsem.at[k, s], peers[k]
+        )
+
+    for s in range(2):
+        for k, head in enumerate(targets):
+            if s == 0:
+                for load in loads[k]:
+                    load.wait()
+            value = dot(
+                x_ref[s * span : (s + 1) * span, :], wf_ref[:, 3 * k * HD : 3 * (k + 1) * HD]
+            )
+            for i in range(3):
+                part = (value[:, i * HD : (i + 1) * HD] + bias_ref[i, head]).astype(BF16)
+                if k < 3:
+                    psend[k, s, i] = part
+                else:
+                    qkv_ref[i, s, here, :] = part
+            if k < 3:
+                project_copy(k, s).start()
+    load_wf.start()
+    for copy in id_copies:
+        copy.wait()
+
+    mine = tile_at(c, HD)
+    scale = HD ** (-0.5)
+
+    def attended_copy(k, s):
+        return remote(
+            osend.at[k, s],
+            o_ref.at[pl.ds(s * span, span), mine],
+            ossem.at[k, s],
+            orsem.at[k, s],
+            peers[k],
+        )
+
+    def receive(s):
+        def run():
+            for k in range(3):
+                project_copy(k, s).wait_recv()
+
+        return run
+
+    def attend_block(s, k):
+        def run():
+            rows = tile_at(targets[k], span)
+            key_row = jnp.concatenate(
+                [all_ids_ref[d, cc, s : s + 1, :] for cc in range(4)], axis=1
+            ).astype(F32)
+            own = id_columns(all_ids_ref[d, targets[k], s : s + 1, :].astype(F32))
+            score = dot_nt(qkv_ref[0, s, rows, :], qkv_ref[1, s]) * scale
+            score = jnp.where(own == key_row, score, -1e30)
+            top = jnp.max(score, axis=-1, keepdims=True)
+            lse = top + jnp.log(jnp.sum(jnp.exp(score - top), axis=-1, keepdims=True))
+            lse_ref[s, rows, :] = lse
+            weights = jnp.exp(score - lse).astype(BF16)
+            block = dot(weights, qkv_ref[2, s]).astype(BF16)
+            if k < 3:
+                osend[k, s] = block
+                attended_copy(k, s).start()
+            else:
+                o_ref[s * span : (s + 1) * span, mine] = block
+
+        return run
+
+    def attended(s):
+        def run():
+            for k in range(3):
+                attended_copy(k, s).wait_recv()
+
+        return run
+
+    columns = width // (2 * PIECES)
+
+    def columns_at(half, piece):
+        return tile_at(half * PIECES + piece, columns)
+
+    def of_attention(s):
+        return lambda half, piece: dot(
+            o_ref[s * span : (s + 1) * span, :], wo_ref[:, columns_at(half, piece)]
+        )
+
+    def of_hidden(s):
+        return lambda half, piece: dot(
+            act_ref[s * span : (s + 1) * span, :], wf_ref[:, columns_at(half, piece)]
+        )
+
+    def of_back(s):
+        return lambda half, piece: dot_nt(
+            slope_ref[s * span : (s + 1) * span, :], wi_ref[columns_at(half, piece), :]
+        )
+
+    count = len(refs) - SCATTER_REFS
+    sets = (refs[: count // 2], refs[count // 2 : count])
+    produces = [make(s) for make in (of_attention, of_hidden, of_back) for s in range(2)]
+    lines = [Line(sets[k % 2], produce) for k, produce in enumerate(produces)]
+
+    def first_norm(s):
+        line = lines[s]
+
+        def run():
+            line.arrived()
+
+            def body(start):
+                rows = pl.ds(s * span + start, STEP_ROWS)
+                first = x_ref[rows, :].astype(F32) + (line.rows(start) + vec_ref[0:1, :])
+                center = first - mean_last(first)
+                rstd = lax.rsqrt(mean_last(center * center) + 1e-05)
+                value = center * rstd
+                norm_ref[rows, :] = value.astype(BF16)
+                rstd_ref[rows, :] = rstd
+                low_ref[rows, :] = (value * vec_ref[1:2, :] + vec_ref[2:3, :]).astype(BF16)
+
+            each_block(span, body)
+
+        return run
+
+    block = 256
+
+    def up(s, first, last):
+        rows = slice(s * span, (s + 1) * span)
+
+        def run():
+            def body(j, carry):
+                cols = tile_at(j, block)
+                u = dot(low_ref[rows, :], wi_ref[:, cols]) + bi_ref[0:1, cols]
+                square = u * u
+                th = jnp.tanh(GELU_A * (u + 0.044715 * (u * square)))
+                act_ref[rows, cols] = (0.5 * u * (1.0 + th)).astype(BF16)
+                slope_ref[rows, cols] = (
+                    0.5 * (1.0 + th)
+                    + 0.5 * u * (1.0 - th * th) * (GELU_A * (1.0 + 3.0 * 0.044715 * square))
+                ).astype(BF16)
+                return carry
+
+            lax.fori_loop(first, last, body, 0)
+
+        return run
+
+    def second_norm(s):
+        line = lines[2 + s]
+
+        def run():
+            line.arrived()
+            total_count = jnp.sum((all_ids_ref[...] > 0).astype(F32))
+            factor = 2.0 * (2 * 4 * 2 * span) / total_count
+
+            def body(start):
+                rows = pl.ds(s * span + start, STEP_ROWS)
+                second = norm_ref[rows, :].astype(F32) * vec_ref[1:2, :] + vec_ref[2:3, :]
+                second = second + (line.rows(start) + vec_ref[3:4, :])
+                center = second - mean_last(second)
+                rstd = lax.rsqrt(mean_last(center * center) + 1e-05)
+                value = center * rstd
+                result = value * vec_ref[4:5, :] + vec_ref[5:6, :]
+                x_ref[rows, :] = result.astype(BF16)
+                gap = (result - mix_ref[rows, :].astype(F32)) * valid_ref[rows, :]
+                error_ref[...] += fold(gap * gap)
+                d_result = gap * factor
+                sums_ref[0] += fold(d_result * value)
+                sums_ref[1] += fold(d_result)
+                d_value = d_result * vec_ref[4:5, :]
+                d_second = (d_value - mean_last(d_value) - value * mean_last(d_value * value)) * rstd
+                d_low = d_second.astype(BF16)
+                dlow_ref[rows, :] = d_low
+                sums_ref[2] += fold(d_low.astype(F32))
+
+            each_block(span, body)
+
+        return run
+
+    def down(s, first, last):
+        rows = slice(s * span, (s + 1) * span)
+
+        def run():
+            def body(j, carry):
+                cols = tile_at(j, block)
+                d_act = dot_nt(dlow_ref[rows, :], wf_ref[cols, :])
+                d_pre = (d_act * slope_ref[rows, cols].astype(F32)).astype(BF16)
+                slope_ref[rows, cols] = d_pre
+                bsum_ref[:, cols] += fold(d_pre.astype(F32))
+                return carry
+
+            lax.fori_loop(first, last, body, 0)
+
+        return run
+
+    def first_back(s):
+        line = lines[4 + s]
+
+        def run():
+            line.arrived()
+
+            def body(start):
+                rows = pl.ds(s * span + start, STEP_ROWS)
+                value = norm_ref[rows, :].astype(F32)
+                d_normed = dlow_ref[rows, :].astype(F32) + line.rows(start)
+                sums_ref[3] += fold(d_normed * value)
+                sums_ref[4] += fold(d_normed)
+                d_value = d_normed * vec_ref[1:2, :]
+                d_first = d_value - mean_last(d_value) - value * mean_last(d_value * value)
+                d_low = (d_first * rstd_ref[rows, :]).astype(BF16)
+                mix_ref[rows, :] = d_low
+                sums_ref[5] += fold(d_low.astype(F32))
+
+            each_block(span, body)
+
+        return run
+
+    narrow = gouter_ref.shape[1]
+    tall = refs[count].shape[2]
+
+    def outer_tile(core, ctx, tile):
+        return dot_tn(act_ref[:, tile_at(tile, tall)], dlow_ref[:, tile_at(core * 4 + ctx, narrow)])
+
+    def outer_write(tile, value):
+        gouter_ref[tile_at(tile, tall), :] = value
+
+    outer = Scatter(
+        outer_tile, lambda tile: gouter_ref[tile_at(tile, tall), :], outer_write, refs[count:]
+    )
+    pairs = outer.pairs()
+    receive(0)()
+    for k in range(4):
+        attend_block(0, k)()
+    attended(0)()
+    load_wo.wait()
+    pieces = local // block
+    a, b, e = 2 * pieces // 8, 5 * pieces // 8, pieces
+    tasks = [
+        [(0, receive(1))] + [(k, attend_block(1, k)) for k in range(4)] + [(7, attended(1))],
+        [(4, first_norm(0)), (5, load_wi.wait), (5, up(0, 0, a)), (6, up(0, a, b)), (7, up(0, b, e)), (7, lines[0].drain), (7, load_wf.wait)],
+        [(4, first_norm(1)), (5, up(1, 0, a)), (6, up(1, a, b)), (7, up(1, b, e)), (7, lines[1].drain), (3, load_teacher.wait)],
+        [(4, second_norm(0)), (5, down(0, 0, a)), (6, down(0, a, b)), (7, down(0, b, e)), (7, lines[2].drain)],
+        [(4, second_norm(1)), (5, down(1, 0, a)), (5, lambda: outer.give(0)), (6, down(1, a, b)), (6, pairs[0]), (7, down(1, b, e)), (7, lines[3].drain)],
+        [(0, pairs[1]), (1, pairs[2]), (2, pairs[3]), (4, first_back(0)), (7, lines[4].drain)],
+    ]
+    run_stream(lines, tasks)
+    stores = [
+        pltpu.make_async_copy(qkv_ref, qkv_hbm, lsem.at[0]),
+        pltpu.make_async_copy(o_ref, o_hbm, lsem.at[1]),
+        pltpu.make_async_copy(low_ref, low_hbm, lsem.at[2]),
+        pltpu.make_async_copy(x_ref, out_hbm, lsem.at[3]),
+        pltpu.make_async_copy(slope_ref, dpre_hbm, lsem.at[4]),
+    ]
+    for store in stores:
+        store.start()
+    first_back(1)()
+    store_mix = pltpu.make_async_copy(mix_ref, dmix_hbm, lsem.at[5])
+    store_mix.start()
+    lines[5].drain()
+    outer.finish()
+    store_outer = pltpu.make_async_copy(gouter_ref, gouter_hbm, lsem.at[6])
+    store_outer.start()
+    for k in range(3):
+        for s in range(2):
+            project_copy(k, s).wait_send()
+            attended_copy(k, s).wait_send()
+    for store in stores + [store_mix, store_outer]:
+        store.wait()
+
+
+def forward(inputs, ids, valid, w_query, w_key, w_value, bias, w_output, w_inner, b_inner, w_outer, teacher, vectors):
+    seqs, span = ids.shape
+    rows, width = inputs.shape
+    local = w_inner.shape[1]
+    heads = w_output.shape[0]
+    length = 4 * span
+    vmem = pl.BlockSpec(memory_space=pltpu.VMEM)
+    hbm = pl.BlockSpec(memory_space=pl.ANY)
+    shape = jax.ShapeDtypeStruct
+    semaphores = pltpu.SemaphoreType.DMA
+    return pl.pallas_call(
+        forward_kernel,
+        out_shape=(
+            shape((2, 4, seqs, span), jnp.int32),
+            shape((3, seqs, length, HD), BF16),
+            shape((seqs, length, 1), F32),
+            shape((rows, heads), BF16),
+            shape((rows, width), BF16),
+            shape((rows, width), BF16),
+            shape((rows, local), BF16),
+            shape((rows, width), BF16),
+            shape((6, 8, width), F32),
+            shape((8, local), F32),
+            shape((8, width), F32),
+            shape((local, width // 8), F32),
+        ),
+        in_specs=[hbm, vmem, vmem, hbm, hbm, hbm, vmem, hbm, hbm, vmem, hbm, hbm, vmem],
+        out_specs=(vmem, hbm, vmem, hbm, hbm, hbm, hbm, hbm, vmem, vmem, vmem, hbm),
+        scratch_shapes=[
+            pltpu.VMEM((rows, width), BF16),
+            pltpu.VMEM((local, width), BF16),
+            pltpu.VMEM((width, local), BF16),
+            pltpu.VMEM((heads, width), BF16),
+            pltpu.VMEM((3, seqs, length, HD), BF16),
+            pltpu.VMEM((3, seqs, 3, span, HD), BF16),
+            pltpu.VMEM((rows, heads), BF16),
+            pltpu.VMEM((3, seqs, span, HD), BF16),
+            pltpu.VMEM((rows, width), BF16),
+            pltpu.VMEM((rows, 1), F32),
+            pltpu.VMEM((rows, width), BF16),
+            pltpu.VMEM((rows, local), BF16),
+            pltpu.VMEM((rows, local), BF16),
+            pltpu.VMEM((rows, width), BF16),
+            pltpu.VMEM((rows, width), BF16),
+            pltpu.VMEM((local, width // 8), F32),
+            semaphores((7,)),
+            semaphores((4, 3)),
+            semaphores((3, seqs)),
+            semaphores((3, seqs)),
+            semaphores((7,)),
+            semaphores((7,)),
+            semaphores((3, seqs)),
+            semaphores((3, seqs)),
+        ]
+        + stream_scratch(span, width)
+        + stream_scratch(span, width)
+        + scatter_scratch(4, local // 4, width // 8),
+        compiler_params=pltpu.CompilerParams(
+            collective_id=0, has_side_effects=True, vmem_limit_bytes=VMEM_BYTES
+        ),
+        name="forward",
+    )(inputs, ids, valid, w_query, w_key, w_value, bias, w_output, w_inner, b_inner, w_outer, teacher, vectors)
+
+
+def attend_back_kernel(
+    dmix_ref, wo_ref, qkv_ref, lse_ref, ids_ref, wq_hbm, wk_hbm, wv_hbm, sums_ref, bsum_ref, error_ref, o_ref, x_ref, low_ref, dpre_hbm,
+    grad_hbm, small_ref, loss_ref, goutput_ref, gqkv_ref, ginner_ref,
+    drows_ref, dpre_ref, d_all, dsend, dkv, gsend, w_refs, stage, pack, packs, lsem, gsem, ssem, rsem, gssem, grsem, pssem, prsem,
+    *refs,
+):
+    d, c, t = place()
+    line, refs = refs[:LINE_REFS], refs[LINE_REFS:]
+    loads = [
+        pltpu.make_async_copy(ref, w_refs.at[i], lsem.at[i])
+        for i, ref in enumerate((wq_hbm, wk_hbm, wv_hbm))
+    ] + [
+        pltpu.make_async_copy(dpre_hbm, dpre_ref, lsem.at[3]),
+    ]
+    for load in loads:
+        load.start()
+    span = dmix_ref.shape[0] // 2
+    peers = ctx_peers()
+    others = peers + [(1 - d, cc, t) for cc in (peers[0][1], peers[1][1], peers[2][1], c)]
+    greet(others, True)
+    targets = [peer[1] for peer in peers] + [c]
+    mine = pl.ds(pl.multiple_of(c * HD, HD), HD)
+    here = pl.ds(pl.multiple_of(c * span, span), span)
+    copies = []
+    for k, target in enumerate(targets):
+        wide = wo_ref[pl.ds(pl.multiple_of(target * HD, HD), HD), :]
+        for s in range(2):
+            block = dot_nt(dmix_ref[s * span : (s + 1) * span, :], wide).astype(BF16)
+            if k < 3:
+                dsend[k, s] = block
+            else:
+                d_all[s, here, :] = block
+        if k < 3:
+            copy = remote(dsend.at[k], d_all.at[:, here, :], ssem.at[k], rsem.at[k], peers[k])
+            copy.start()
+            copies.append(copy)
+    narrow = goutput_ref.shape[1]
+
+    def output_write(tile, value):
+        goutput_ref[...] = value
+
+    output = Scatter(
+        lambda core, ctx, tile: dot_tn(o_ref[...], dmix_ref[:, tile_at(core * 4 + ctx, narrow)]),
+        lambda tile: goutput_ref[...],
+        output_write,
+        refs[:SCATTER_REFS],
+    )
+    output.give(0)
+    for task in output.pairs():
+        task()
+    for copy in copies:
+        copy.wait()
+    scale = HD ** (-0.5)
+    copies = []
+    for s in range(2):
+        rows_here = pl.ds(s * span, span)
+        key_row = jnp.concatenate([ids_ref[d, cc, s : s + 1, :] for cc in range(4)], axis=1)
+        keys = qkv_ref[1, s]
+        values = qkv_ref[2, s]
+        for k, target in enumerate(targets):
+            rows = pl.ds(pl.multiple_of(target * span, span), span)
+            own = id_columns(ids_ref[d, target, s : s + 1, :].astype(F32))
+            queries = qkv_ref[0, s, rows, :]
+            score = dot_nt(queries, keys) * scale
+            score = jnp.where(own == key_row.astype(F32), score, -1e30)
+            probs = jnp.exp(score - lse_ref[s, rows, :])
+            d_out = d_all[s, rows, :]
+            d_probs = dot_nt(d_out, values)
+            inner = jnp.sum(probs * d_probs, axis=-1, keepdims=True)
+            d_score = (probs * (d_probs - inner)).astype(BF16)
+            d_query = (dot(d_score, keys) * scale).astype(BF16)
+            d_key = dot_tn(d_score, queries)
+            d_value = dot_tn(probs.astype(BF16), d_out)
+            if k == 0:
+                dkv[0] = d_key
+                dkv[1] = d_value
+            else:
+                dkv[0] += d_key
+                dkv[1] += d_value
+            if k < 3:
+                gsend[0, k, s] = d_query
+                copy = remote(
+                    gsend.at[0, k, s],
+                    drows_ref.at[0, rows_here, mine],
+                    gssem.at[0, k, s],
+                    grsem.at[0, k, s],
+                    peers[k],
+                )
+                copy.start()
+                copies.append(copy)
+            else:
+                drows_ref[0, rows_here, mine] = d_query
+        for k, target in enumerate(targets):
+            rows = pl.ds(pl.multiple_of(target * span, span), span)
+            for i, factor in ((0, scale), (1, 1.0)):
+                block = (dkv[i, rows, :] * factor).astype(BF16)
+                if k < 3:
+                    gsend[1 + i, k, s] = block
+                    copy = remote(
+                        gsend.at[1 + i, k, s],
+                        drows_ref.at[1 + i, rows_here, mine],
+                        gssem.at[1 + i, k, s],
+                        grsem.at[1 + i, k, s],
+                        peers[k],
+                    )
+                    copy.start()
+                    copies.append(copy)
+                else:
+                    drows_ref[1 + i, rows_here, mine] = block
+    for copy in copies:
+        copy.wait()
+    for i in range(6):
+        pack[i : i + 1, :] = jnp.sum(sums_ref[i], axis=0, keepdims=True)
+    pack[6:7, :] = jnp.sum(bsum_ref[...], axis=0, keepdims=True)
+    lanes = drows_ref.shape[2]
+    pack[7:8, 0:lanes] = jnp.sum(drows_ref[0].astype(F32), axis=0, keepdims=True)
+    pack[7:8, lanes : 2 * lanes] = jnp.sum(drows_ref[2].astype(F32), axis=0, keepdims=True)
+    error = jnp.sum(error_ref[...])
+    pack[7:8, 2 * lanes : 4 * lanes] = jnp.full((1, 2 * lanes), error, F32)
+    small_copies = []
+    for i, other in enumerate(others):
+        copy = remote(pack, packs.at[d, c], pssem.at[i], prsem.at[i], other)
+        copy.start()
+        small_copies.append(copy)
+    for load in loads:
+        load.wait()
+    columns = line[3].shape[3]
+
+    def produce(half, chunk):
+        cols = pl.ds(pl.multiple_of(chunk * columns, columns), columns)
+        rows = tile_at(half, span)
+        return (
+            dot_nt(drows_ref[0, rows, :], w_refs[0, cols, :])
+            + dot_nt(drows_ref[1, rows, :], w_refs[1, cols, :])
+            + dot_nt(drows_ref[2, rows, :], w_refs[2, cols, :])
+        )
+
+    deep = gqkv_ref.shape[1]
+
+    def qkv_write(tile, value):
+        gqkv_ref[tile] = value
+
+    qkv_grad = Scatter(
+        lambda core, ctx, tile: dot_tn(x_ref[:, tile_at(core * 4 + ctx, deep)], drows_ref[tile]),
+        lambda tile: gqkv_ref[tile],
+        qkv_write,
+        refs[SCATTER_REFS : 2 * SCATTER_REFS],
+    )
+    wide = refs[2 * SCATTER_REFS].shape[3]
+
+    def inner_tile(core, ctx, tile):
+        return dot_tn(low_ref[:, tile_at(core * 4 + ctx, deep)], dpre_ref[:, tile_at(tile, wide)])
+
+    def inner_write(tile, value):
+        ginner_ref[:, tile_at(tile, wide)] = value
+
+    inner = Scatter(
+        inner_tile,
+        lambda tile: ginner_ref[:, tile_at(tile, wide)],
+        inner_write,
+        refs[2 * SCATTER_REFS :],
+    )
+    qkv_grad.give(0)
+    tasks = list(enumerate(qkv_grad.pairs())) + [(3, lambda: inner.give(0))]
+    tasks += [(4 + i, task) for i, task in enumerate(inner.pairs())]
+    line_sum(produce, line, tasks)
+
+    def finish(step, carry):
+        rows = rows_at(step)
+        slot = lax.rem(step, 2)
+
+        def store(at):
+            return pltpu.make_async_copy(stage.at[slot], grad_hbm.at[rows_at(at), :], gsem.at[slot])
+
+        @pl.when(step >= 2)
+        def _():
+            store(step - 2).wait()
+
+        stage[slot] = dmix_ref[rows, :].astype(F32) + row_block(line[3], step)
+        store(step).start()
+        return carry
+
+    steps = dmix_ref.shape[0] // STEP_ROWS
+    lax.fori_loop(0, steps, finish, 0)
+    for i in range(2):
+        pltpu.make_async_copy(
+            stage.at[i], grad_hbm.at[pl.ds((steps - 2 + i) * STEP_ROWS, STEP_ROWS), :], gsem.at[i]
+        ).wait()
+    output.finish()
+    qkv_grad.finish()
+    inner.finish()
+    for copy in small_copies:
+        copy.wait()
+    packs[d, c] = pack[...]
+    small = jnp.zeros_like(pack)
+    for i in range(2):
+        for j in range(4):
+            small = small + packs[i, j]
+    small_ref[...] = small
+    count = jnp.sum((ids_ref[...] > 0).astype(F32))
+    loss_ref[...] = jnp.broadcast_to(small[7:8, 2 * lanes : 2 * lanes + 128] / count, (8, 128))
+
+
+def attend_back(
+    d_mix, w_output, qkv, lse, all_ids, w_query, w_key, w_value, sums, inner_sum, error, attn_rows, inputs, low, d_pre
+):
+    rows, width = d_mix.shape
+    local = w_query.shape[1]
+    seqs, length = qkv.shape[1], qkv.shape[2]
+    span = rows // seqs
+    vmem = pl.BlockSpec(memory_space=pltpu.VMEM)
+    hbm = pl.BlockSpec(memory_space=pl.ANY)
+    return pl.pallas_call(
+        attend_back_kernel,
+        out_shape=(
+            jax.ShapeDtypeStruct((rows, width), F32),
+            jax.ShapeDtypeStruct((8, width), F32),
+            jax.ShapeDtypeStruct((8, 128), F32),
+            jax.ShapeDtypeStruct((local, width // 8), F32),
+            jax.ShapeDtypeStruct((3, width // 8, local), F32),
+            jax.ShapeDtypeStruct((width // 8, d_pre.shape[1]), F32),
+        ),
+        in_specs=[vmem] * 5 + [hbm] * 3 + [vmem] * 6 + [hbm],
+        out_specs=(hbm,) + (vmem,) * 5,
+        scratch_shapes=[
+            pltpu.VMEM((3, rows, local), BF16),
+            pltpu.VMEM((rows, d_pre.shape[1]), BF16),
+            pltpu.VMEM((seqs, length, HD), BF16),
+            pltpu.VMEM((3, seqs, span, HD), BF16),
+            pltpu.VMEM((2, length, HD), F32),
+            pltpu.VMEM((3, 3, seqs, span, HD), BF16),
+            pltpu.VMEM((3, width, local), BF16),
+            pltpu.VMEM((2, STEP_ROWS, width), F32),
+            pltpu.VMEM((8, width), F32),
+            pltpu.VMEM((2, 4, 8, width), F32),
+            pltpu.SemaphoreType.DMA((4,)),
+            pltpu.SemaphoreType.DMA((2,)),
+            pltpu.SemaphoreType.DMA((3,)),
+            pltpu.SemaphoreType.DMA((3,)),
+            pltpu.SemaphoreType.DMA((3, 3, seqs)),
+            pltpu.SemaphoreType.DMA((3, 3, seqs)),
+            pltpu.SemaphoreType.DMA((7,)),
+            pltpu.SemaphoreType.DMA((7,)),
+        ]
+        + line_scratch(rows, width)
+        + scatter_scratch(1, local, width // 8)
+        + scatter_scratch(3, width // 8, local)
+        + scatter_scratch(4, width // 8, d_pre.shape[1] // 4),
+        compiler_params=pltpu.CompilerParams(
+            collective_id=4, has_side_effects=True, vmem_limit_bytes=VMEM_BYTES
+        ),
+        name="attend_back",
+    )(
+        d_mix, w_output, qkv, lse, all_ids, w_query, w_key, w_value, sums, inner_sum, error, attn_rows, inputs, low, d_pre
+    )
+
+
+def quick_shards(
+    hidden_in,
+    segment_ids,
+    teacher,
+    w_query,
+    b_query,
+    w_key,
+    w_value,
+    b_value,
+    w_output,
+    b_output,
+    first_gain,
+    first_shift,
+    w_inner,
+    b_inner,
+    w_outer,
+    b_outer,
+    second_gain,
+    second_shift,
+):
+    seq_count, span_len, width = hidden_in.shape
+    rows = seq_count * span_len
+    local = w_query.shape[1]
+    inputs = hidden_in.reshape(rows, width)
+    bias = jnp.stack([b_query, jnp.zeros_like(b_query), b_value]).reshape(3, local // HD, 1, HD)
+    valid = (segment_ids.reshape(rows, 1) > 0).astype(F32)
+    vectors = jnp.stack([b_output, first_gain, first_shift, b_outer, second_gain, second_shift])
+    (
+        all_ids,
+        qkv,
+        lse,
+        attn_rows,
+        normed_low,
+        layer_out,
+        d_pre,
+        d_mix,
+        sums,
+        inner_sum,
+        error,
+        grad_w_outer,
+    ) = forward(
+        inputs,
+        segment_ids,
+        valid,
+        w_query,
+        w_key,
+        w_value,
+        bias,
+        w_output,
+        w_inner,
+        b_inner.reshape(1, -1),
+        w_outer,
+        teacher.reshape(rows, width),
+        vectors,
+    )
+    grad_input, small, loss, grad_w_output, grad_qkv, grad_w_inner = attend_back(
+        d_mix,
+        w_output,
+        qkv,
+        lse,
+        all_ids,
+        w_query,
+        w_key,
+        w_value,
+        sums,
+        inner_sum,
+        error,
+        attn_rows,
+        inputs,
+        normed_low,
+        d_pre,
+    )
+    grad_w_query, grad_w_key, grad_w_value = grad_qkv[0], grad_qkv[1], grad_qkv[2]
+    shape = (seq_count, span_len, width)
+    return (
+        layer_out.reshape(shape),
+        loss[0, 0],
+        grad_input.reshape(shape),
+        grad_w_query,
+        small[7, :local],
+        grad_w_key,
+        grad_w_value,
+        small[7, local : 2 * local],
+        grad_w_output,
+        small[5],
+        small[3],
+        small[4],
+        grad_w_inner,
+        small[6],
+        grad_w_outer,
+        small[2],
+        small[0],
+        small[1],
+    )
+
+
+def chosen(*args):
+    seq_count, span_len, width = args[0].shape
+    local_heads = args[3].shape[1] // HD
+    fits = (
+        seq_count == 2
+        and lax.axis_size("dp") == 2
+        and lax.axis_size("ctx") == 4
+        and local_heads == 4
+        and args[12].shape[1] == width
+        and 4 * args[3].shape[1] == width
+    )
+    return quick_shards(*args) if fits else shards(*args)
+
+
 def solution(mesh):
     placed = (
         P("dp", "ctx", None),
@@ -265,7 +1504,7 @@
         P(),
     )
     return jax.shard_map(
-        shards,
+        chosen,
         mesh=mesh,
         in_specs=placed,
         out_specs=(

time: 1400 us -> 383 us (0.27)
  waiting for transfers between devices: 1100 us -> 0 us
  Pallas kernels: 0 us -> 353 us
  matrix products: 122 us -> 0 us
  blocking collectives: 66.9 us -> 0 us
  other arithmetic: 47.2 us -> 2.05 us
  local copies, waits for them, and re-layouts: 37.1 us -> 19.5 us
  between operations: 17.8 us -> 0.92 us
    psum x4 -> x0, waiting for transfers between devices: 561 us -> none  [the longest x1 155 us: shards(): lax.psum(jnp.dot(attn_rows, w_output, preferred_element_type=jnp.float32)...]
    reduce_scatter x8 -> x0, waiting for transfers between devices: 490 us -> none  [the longest x1 120 us: shards(): lax.psum_scatter(grad_w_inner, ('dp', 'ctx'), scatter_dimension=0, tiled=...]
    pallas_call x0 -> x2, Pallas kernels: none -> 353 us  [the longest x1 220 us: forward(): pl.pallas_call(forward_kernel, out_shape=(shape((2, 4, seqs, span), jnp.i...]
    dot_general x32 -> x0, matrix products: 122 us -> none  [the longest x6 35.4 us: outer_sum(): jnp.einsum('rd,re->de', left, right, preferred_element_type=jnp.float32)]
    psum x3 -> x0, blocking collectives: 57.3 us -> none  [the longest x2 30.5 us: shards(): lax.psum((jnp.sum(valid_rows[:, None] * error_gap * error_gap), jnp.sum(v...]
    all_gather x2 -> x0, waiting for transfers between devices: 53.9 us -> none  [the longest x1 33.7 us: shards(): lax.all_gather(value_local, 'ctx', axis=1, tiled=True)]
    reduce_sum x15 -> x0, other arithmetic: 30.9 us -> none  [the longest x4 12.8 us: layer_norm(): center = values - jnp.mean(values, axis=-1, keepdims=True)]
  transfers between devices with their start and end apart: 14 -> 0, of which waited for: 13 -> 0; matrix products, arithmetic and copies ran while one was open for 6% -> 0% of each run, Pallas kernels for 0% -> 0%
where the time goes in v1:
time: 383 us; the launch traced here: 376 us
  Pallas kernels  353 us (92%)
  local copies, waits for them, and re-layouts  19.5 us (5%)
    pallas_call x1, Pallas kernels, forward(): pl.pallas_call(forward_kernel, out_shape=(shape((2, 4, seqs, span), jnp.i...  220 us
    pallas_call x1, Pallas kernels, attend_back(): pl.pallas_call(attend_back_kernel, out_shape=(jax.ShapeDtypeStruct((rows,...  134 us
    unnamed x17, local copies, waits for them, and re-layouts  10.9 us

profile of v1, /device:TPU:0, one launch (start us, length us, event | category | flops | bytes accessed | tf_op | source)
XLA Modules:
  0.0 375.7 jit_solution(7781251498217339400)
XLA Ops:
  0.7 0.1 pad.1.clone
  0.7 0.7 fusion
  1.4 1.4 pad_maximum_fusion.bias_ref
  2.8 1.5 stack.39.vec_ref
  4.3 0.9 copy.38
  5.1 219.6 %forward.1 = (s32[2,4,2,256]{3,2,1,0:T(2,128)}, bf16[3,2,1024,128]{3,2,1,0:T(8,128)(2,1)}, f32[2,1024,1]{2,1,0:T(8,128)}, bf16[512,512]{1,0:T(8,128)(2,1)}, bf16...) custom-call(bf16[512,2048]{1,0:T(8,128)(2,1)} %bitcast.35, ...), custom_call_target="tpu_custom_call" | custom-call | tf_op jit(solution)/shard_map/forward/pallas_call | solution.py:1064
  224.8 133.6 %attend_back.1 = (f32[512,2048]{1,0:T(8,128)}, f32[8,2048]{1,0:T(8,128)}, f32[8,128]{1,0:T(8,128)}, f32[512,256]{1,0:T(8,128)}, f32[3,256,512]{2,1,0:T(8,128)}, /*index=5*/f32[256,2048]{1,0:T(8,128)}) custom-call(bf16[512,2048]{1,0:T(8,128)(2,1)} %get-tuple-element.37.dmix_ref, bf16[512,2048]{1,0:T(8,128)(2,1)} %wo_ref.1, ...), custom_call_target="tpu_custom_call" | custom-call | tf_op jit(solution)/shard_map/attend_back/pallas_call | solution.py:1330
  358.4 0.0 copy-start.2
  358.4 1.3 slice.39
  359.8 1.3 fusion.2
  361.1 1.8 fusion.1
  362.9 2.5 slice_bitcast_fusion
  365.4 0.0 copy-done.2
  365.4 0.0 copy-start
  365.4 1.3 copy.44
  366.8 1.6 copy-done
  368.4 0.0 copy-start.4
  368.4 0.0 copy-start.3
  368.4 2.1 copy.45
  370.5 0.0 copy-done.4
  370.5 0.8 copy.46
  371.3 0.5 copy-done.3
  371.9 0.0 copy-start.1
  371.9 1.3 copy.47
  373.2 1.0 copy-done.1
  374.2 1.3 copy.48
  (1 shorter events, 0.0 us)
Async XLA Ops:
  358.4 7.0 %copy-start.2 = (bf16[512,2048]{1,0:T(8,128)(2,1)S(1)}, bf16[512,2048]{1,0:T(8,128)(2,1)}, u32[]{:S(2)}) copy-start(bf16[512,2048]{1,0:T(8,128)(2,1)} %get-tuple-element.36) | copy-start | bytes 6291460
  365.4 2.9 copy-start
  368.4 2.1 copy-start.4
  368.4 3.5 copy-start.3
  371.9 2.3 copy-start.1
